TPU v7x, 128 devices: a whole 4x4x4 slice. The times are simulated.
128 devices in a mesh: row: 8 (over x, y_lo), col: 16 (over y_hi, z, core).
Axes of the slice: x: 4, y: 4 (y_hi: 2, y_lo: 2; y = y_hi * 2 + y_lo), z: 4, core: 2. Of those that a mesh axis runs over, the one named last changes fastest.
Arguments:
- front: float32 [10240, 10240], P('row', 'col'), as said below
- updates: float32 [16384, 8192], P('row', 'col'), as said below
- maps: int32 [2, 64], replicated, may hold values from 0 to 79, as said below
Outputs:
- panel_factor: float32 [10240, 2048], P('row', 'col')
- trailing: float32 [10240, 10240], P('row', 'col')
Inputs may be any that keep to these rules, and one draw needn't show every extreme that they name: `maps`: each row lists 64 distinct front blocks; entry j leaves remainder floor(j / 4) on division by 16, the entries of one remainder rise with j, and blocks 0 and 79 appear in both rows. Symmetric in front order; the assembled leading 2048 x 2048 block is positive definite. `updates`: each child's update is symmetric in the child's own order.
All inputs are finite; a program needn't handle non-finite values.
Results may differ from a plain program's by a relative error of at most 0.0001.
Values sent between devices are 32-bit elements; how exact they have to be, the bound alone decides.
No kernel may reach another device: no remote copies, remote signals or barrier semaphores. Data moves between devices by JAX's collectives and lax.ppermute only.
A program may use at most 192 MiB of HBM per device.

v0:
```python
import jax
import jax.numpy as jnp
from jax import lax
from jax.sharding import PartitionSpec as P

BLK = 128
PW = 2048


def from_root(value, axis, source):
    kept = jnp.where(lax.axis_index(axis) == source, value, 0).astype(value.dtype)
    return lax.psum(kept, axis)


def block_cholesky(leading):
    order = leading.shape[0]
    count = order // BLK
    identity = jnp.eye(BLK, dtype=jnp.float32)
    factor = jnp.zeros((order, order), jnp.float32)
    inverses = []
    for step in range(count):
        start = step * BLK
        column = leading[start:, start : start + BLK]
        if step > 0:
            column = column - jnp.dot(
                factor[start:, :start],
                factor[start : start + BLK, :start].T,
                precision=lax.Precision.HIGHEST,
                preferred_element_type=jnp.float32,
            )
        diag_factor = jnp.linalg.cholesky(column[:BLK])
        inverse = jax.scipy.linalg.solve_triangular(diag_factor, identity, lower=True)
        inverses.append(inverse)
        factor = factor.at[start : start + BLK, start : start + BLK].set(diag_factor)
        if start + BLK < order:
            below = jnp.dot(
                column[BLK:],
                inverse.T,
                precision=lax.Precision.HIGHEST,
                preferred_element_type=jnp.float32,
            )
            factor = factor.at[start + BLK :, start : start + BLK].set(below)
    return (factor, inverses)


def block_solve(factor, inverses, rows_in):
    count = len(inverses)
    result = jnp.zeros(rows_in.shape, jnp.float32)
    for step in range(count):
        start = step * BLK
        target = rows_in[:, start : start + BLK]
        if step > 0:
            target = target - jnp.dot(
                result[:, :start],
                factor[start : start + BLK, :start].T,
                precision=lax.Precision.HIGHEST,
                preferred_element_type=jnp.float32,
            )
        solved = jnp.dot(
            target,
            inverses[step].T,
            precision=lax.Precision.HIGHEST,
            preferred_element_type=jnp.float32,
        )
        result = result.at[:, start : start + BLK].set(solved)
    return result


def local(front, updates, maps):
    rows_n = lax.axis_size("row")
    cols_n = lax.axis_size("col")
    half_rows = rows_n // 2
    row_at = lax.axis_index("row")
    col_at = lax.axis_index("col")
    front_rows, front_cols = front.shape
    row_slots = front_rows // BLK
    col_slots = front_cols // BLK
    col_group = updates.shape[1] // BLK
    depth_slots = col_group // half_rows
    width_slots = cols_n // rows_n
    child_blocks = maps.shape[1]
    outgoing = updates.reshape(width_slots, rows_n, depth_slots * BLK, col_group * BLK)
    incoming = lax.all_to_all(outgoing, "row", split_axis=1, concat_axis=1, tiled=True)
    incoming = incoming.reshape(width_slots, 2, half_rows, depth_slots, BLK, col_group, BLK)
    shape_grid = (width_slots, half_rows, depth_slots)
    grid_w = lax.broadcasted_iota(jnp.int32, shape_grid, 0)
    grid_a = lax.broadcasted_iota(jnp.int32, shape_grid, 1)
    grid_e = lax.broadcasted_iota(jnp.int32, shape_grid, 2)
    block_id = (((grid_w * rows_n + row_at) * depth_slots + grid_e) * half_rows + grid_a).reshape(
        -1
    )
    child_iota = jnp.arange(child_blocks, dtype=jnp.int32)
    assembled = front
    for which_child in range(2):
        child_map = maps[which_child]
        blocks = incoming[:, which_child].reshape(
            width_slots * half_rows * depth_slots, BLK, col_group, BLK
        )
        matched = block_id[:, None] == child_iota[None, :]
        targets = jnp.sum(jnp.where(matched, child_map[None, :], 0), axis=1)
        row_place = (
            targets[None, :] // rows_n == jnp.arange(row_slots, dtype=jnp.int32)[:, None]
        ).astype(jnp.float32)
        col_ids = lax.dynamic_slice_in_dim(child_map, col_at * col_group, col_group)
        col_place = (
            col_ids[None, :] // cols_n == jnp.arange(col_slots, dtype=jnp.int32)[:, None]
        ).astype(jnp.float32)
        placed = jnp.einsum("pn,nxvy->pxvy", row_place, blocks, precision=lax.Precision.HIGHEST)
        placed = jnp.einsum("pxvy,qv->pxqy", placed, col_place, precision=lax.Precision.HIGHEST)
        assembled = assembled + placed.reshape(front_rows, front_cols)
    panel_rslots = PW // BLK // rows_n
    panel_cslots = PW // BLK // cols_n
    gathered = lax.all_gather(assembled[:, : panel_cslots * BLK], "col", axis=1, tiled=True)
    panel_rows = (
        gathered.reshape(front_rows, cols_n, panel_cslots, BLK)
        .transpose(0, 2, 1, 3)
        .reshape(front_rows, PW)
    )
    corner = assembled[: panel_rslots * BLK, : panel_cslots * BLK]
    pieces = lax.all_gather(corner, ("row", "col"), axis=0, tiled=True)
    leading = (
        pieces.reshape(rows_n, cols_n, panel_rslots, BLK, panel_cslots, BLK)
        .transpose(2, 0, 3, 4, 1, 5)
        .reshape(PW, PW)
    )
    factor, inverses = block_cholesky(leading)
    lower_rows = block_solve(factor, inverses, panel_rows[panel_rslots * BLK :])
    head_rows = lax.dynamic_index_in_dim(
        factor.reshape(panel_rslots, rows_n, BLK, PW), row_at, 1, keepdims=False
    )
    factor_rows = jnp.concatenate([head_rows.reshape(panel_rslots * BLK, PW), lower_rows], axis=0)
    col_span = cols_n // rows_n
    root_row = col_at % rows_n
    picked = lax.dynamic_index_in_dim(
        factor_rows.reshape(col_slots, col_span, BLK, PW), col_at // rows_n, 1, keepdims=False
    )
    column_rows = from_root(picked.reshape(col_slots * BLK, PW), "row", root_row)
    update = jnp.dot(
        factor_rows,
        column_rows.T,
        precision=lax.Precision.HIGHEST,
        preferred_element_type=jnp.float32,
    )
    row_keep = jnp.arange(front_rows) // BLK >= panel_rslots
    col_keep = jnp.arange(front_cols) // BLK >= panel_cslots
    trailing = jnp.where(
        row_keep[:, None] & col_keep[None, :], assembled - update, jnp.float32(0.0)
    )
    panel_out = lax.dynamic_index_in_dim(
        factor_rows.reshape(front_rows, panel_cslots, cols_n, BLK), col_at, 2, keepdims=False
    )
    return (panel_out.reshape(front_rows, panel_cslots * BLK), trailing)


def solution(mesh):
    in_specs = (P("row", "col"), P("row", "col"), P())
    out_specs = (P("row", "col"), P("row", "col"))
    return jax.shard_map(local, mesh=mesh, in_specs=in_specs, out_specs=out_specs, check_vma=False)
```

profile of v0, /device:TPU:1, one launch (start us, length us, event | category | flops | bytes accessed | tf_op | source)
XLA Modules:
  0.0 1348.0 jit_solution(4815525074434272048)
XLA Ops:
  18.3 58.4 %all-to-all-done = f32[2,8,128,512]{3,2,0,1:T(8,128)} async-done(((f32[2,8,128,512]{3,2,0,1:T(8,128)}), f32[2,8,128,512]{3,2,0,1:T(8,128)}, u32[]{:S(2)}, u32[]{:S(2)}) %all-to-all-start) | async-done | bytes 4194336 | tf_op jit(solution)/shard_map/all_to_all | solution.py:83
  108.5 208.8 %all-gather.3.cloned.1.call-done = f32[32768,128]{1,0:T(8,128)} async-done(((f32[256,128]{1,0:T(8,128)}), f32[32768,128]{1,0:T(8,128)}) %all-gather.3.cloned.1.call-update) | async-done | bytes 16777232 | tf_op jit(solution)/shard_map/all_gather | solution.py:120
  317.3 17.8 %copy.161 = f32[8,16,2,128,1,128]{3,0,2,5,1,4:T(8,128)} copy(f32[8,16,2,128,1,128]{5,3,2,1,0,4:T(8,128)} %bitcast.269) | data formatting | bytes 33554432 | tf_op jit(solution)/shard_map/reshape | solution.py:122
  335.1 18.0 %reshape.1456 = f32[2048,2048]{0,1:T(8,128)} reshape(f32[2,8,128,1,16,128]{2,1,0,5,4,3:T(8,128)} %bitcast.263) | data formatting | bytes 33554432 | tf_op jit(solution)/shard_map/reshape | solution.py:124
  354.9 11.7 cholesky.254
  368.0 9.8 custom-call.20
  392.2 11.9 cholesky.265
  406.1 9.8 custom-call.21
  422.7 11.7 cholesky.276
  436.4 10.0 custom-call.22
  454.1 11.7 cholesky.287
  467.8 9.8 custom-call.23
  486.3 11.7 cholesky.298
  500.0 9.8 custom-call.24
  518.4 11.7 cholesky.309
  532.2 9.8 custom-call.25
  551.2 11.7 cholesky.320
  564.9 9.8 custom-call.26
  583.7 12.1 cholesky.331
  597.8 9.8 custom-call.27
  616.8 11.9 cholesky.342
  630.6 9.8 custom-call.28
  648.9 11.9 cholesky.353
  662.8 9.8 custom-call.29
  681.0 11.7 cholesky.364
  694.7 10.2 custom-call.30
  712.6 11.7 cholesky.375
  726.3 9.8 custom-call.31
  743.5 11.7 cholesky.386
  757.2 9.8 custom-call.32
  773.1 11.9 cholesky.397
  787.0 9.8 custom-call.33
  802.0 11.7 cholesky.408
  815.7 10.2 custom-call.34
  829.8 11.7 cholesky.419
  850.1 9.8 custom-call.35
  922.8 8.5 fusion.87
  934.4 9.7 fusion.119
  947.1 10.5 fusion.96
  960.8 11.5 fusion.122
  975.4 12.6 fusion.72
  991.0 13.4 fusion.75
  1007.5 14.3 %fusion.125 = f32[1024,128]{1,0:T(8,128)S(1)} fusion(f32[1024,2048]{0,1:T(8,128)} %fusion.100, f32[2048,2048]{1,0:T(8,128)} %get-tuple-element.575, f32[1280,2048]{1,0:T(8,128)S(1)} %bitcast.274), kind=kOutput, calls=%fused_computation.126 | convolution fusion | flops 2818703360 | bytes 9306112 | tf_op jit(solution)/shard_map/dot_general | solution.py:53
  1023.3 14.4 %fusion.78 = f32[1024,128]{1,0:T(8,128)S(1)} fusion(f32[1024,2048]{0,1:T(8,128)S(1)} %fusion.99, f32[2048,2048]{1,0:T(8,128)} %get-tuple-element.575, f32[1280,2048]{1,0:T(8,128)S(1)} %bitcast.274), kind=kOutput, calls=%fused_computation.84 | convolution fusion | flops 3020029952 | bytes 9895936 | tf_op jit(solution)/shard_map/dot_general | solution.py:53
  1048.1 13.3 reshape.1460
  1061.3 21.0 %fusion.10 = f32[5,128,2048]{1,0,2:T(8,128)} fusion(pred[]{:T(512)S(6)} %eq.132, f32[5,2,128,2048]{2,1,0,3:T(2,128)} %reshape.1460, s32[]{:T(128)S(6)} %select_n.110), kind=kLoop, calls=%fused_computation.14 | loop fusion | flops 1310720 | bytes 10485765 | tf_op jit(solution)/shard_map/jit(_where)/select_n | solution.py:11
  1098.3 211.5 %all-reduce.4.cloned.1.call-done = f32[640,2048]{0,1:T(8,128)} async-done(((f32[640,2048]{0,1:T(8,128)}), f32[640,2048]{0,1:T(8,128)}) %all-reduce.4.cloned.1.call-update) | async-done | bytes 5242896 | tf_op jit(solution)/shard_map/psum | solution.py:12
  1309.8 31.6 %fusion.33 = f32[1280,640]{1,0:T(8,128)} fusion(f32[1280,640]{1,0:T(8,128)} %copy-done.5, f32[640,2048]{0,1:T(8,128)} %all-reduce.4.cloned.1.call-done, pred[640]{0:T(1024)(128)(4,1)S(1)} %fusion.278, pred[1280]{0:T(1024)(128)(4,1)S(1)} %fusion.274, f32[1024,2048]{0,1:T(8,128)} %copy-done.1, f32[256,2048]{0,1:T(8,128)S(1)} %copy-done.4), kind=kOutput, calls=%fused_computation.39 | convolution fusion | flops 20137738240 | bytes 22284160 | tf_op jit(solution)/shard_map/dot_general | solution.py:138
  (236 shorter events, 311.6 us)
Async XLA Ops:
  7.2 10.9 copy-start.8
  11.9 64.8 %all-to-all-start = ((f32[2,8,128,512]{3,2,0,1:T(8,128)}), f32[2,8,128,512]{3,2,0,1:T(8,128)}, u32[]{:S(2)}, u32[]{:S(2)}) async-start(f32[2,8,128,512]{3,2,0,1:T(8,128)} %copy.156), calls=%async_computation | async-start | bytes 8388608 | tf_op jit(solution)/shard_map/all_to_all | solution.py:83
  17.8 299.5 %all-gather.3.cloned.1.call-start = ((), (), s32[]{:S(2)}) async-start(), calls=%async_computation.1 | async-start | bytes 16908288 | tf_op jit(solution)/shard_map/all_gather | solution.py:120
  89.3 9.9 copy-start.6
  101.1 234.0 %copy-start.5 = (f32[1280,640]{1,0:T(8,128)}, f32[1280,640]{1,0:T(8,128)S(1)}, u32[]{:S(2)}) copy-start(f32[1280,640]{1,0:T(8,128)S(1)} %bitcast_add_fusion) | copy-start | bytes 9830404
  101.8 741.7 %all-gather.5.cloned.1.call-start = ((), (), s32[]{:S(2)}) async-start(), calls=%async_computation.2 | async-start | bytes 11141120 | tf_op jit(solution)/shard_map/all_gather | solution.py:113
  108.5 1201.3 %all-reduce.4.cloned.1.call-start = ((), (), s32[]{:S(2)}) async-start(), calls=%async_computation.3 | async-start | bytes 10485760 | tf_op jit(solution)/shard_map/psum | solution.py:12
  862.6 35.1 %copy-start.2 = (f32[2,1,128,2048]{3,2,1,0:T(8,128)}, f32[2,1,128,2048]{3,2,1,0:T(8,128)S(1)}, u32[]{:S(2)}) copy-start(f32[2,1,128,2048]{3,2,1,0:T(8,128)S(1)} %constant_dynamic-slice_fusion) | copy-start | bytes 6291460
  875.3 35.9 %slice-start = ((s8[10485760]{0:T(1024)(128)(4,1)}), s8[4194304]{0:T(1024)(128)(4,1)S(1)}, s32[]{:S(2)}) async-start(s8[10485760]{0:T(1024)(128)(4,1)} %bitcast.273), calls=%async_computation.4 | async-start | bytes 8388608
  882.8 28.3 %slice-start.1 = ((s8[10485760]{0:T(1024)(128)(4,1)}), s8[4194304]{0:T(1024)(128)(4,1)S(1)}, s32[]{:S(2)}) async-start(s8[10485760]{0:T(1024)(128)(4,1)} %bitcast.273), calls=%async_computation.5 | async-start | bytes 8388608
  897.7 13.4 slice-start.2
  1007.5 14.4 %copy-start = (f32[1024,2048]{0,1:T(8,128)S(1)}, f32[1024,2048]{0,1:T(8,128)}, u32[]{:S(2)}) copy-start(f32[1024,2048]{0,1:T(8,128)} %fusion.100) | copy-start | bytes 25165828
  1021.8 15.9 %copy-start.7 = (f32[128,128]{1,0:T(8,128)S(1)}, f32[128,128]{1,0:T(8,128)}, u32[]{:S(2)}) copy-start(f32[128,128]{1,0:T(8,128)} %fusion.177) | copy-start | bytes 196612
  1038.3 3.3 copy-start.1
  1082.3 7.2 copy-start.3
  1093.0 216.8 %copy-start.4 = (f32[256,2048]{0,1:T(8,128)S(1)}, f32[256,2048]{0,1:T(8,128)}, u32[]{:S(2)}) copy-start(f32[256,2048]{0,1:T(8,128)} %copy.216) | copy-start | bytes 6291460
Sparse Core Ops, SparseCore 0:
  102.0 215.3 all-gather.2
  320.2 87.1 all-gather.4
  1089.6 220.1 all-reduce.3
where the time goes:
time: 1360 us; the launch traced here: 1350 us
  waiting for transfers between devices  479 us (35%)
  other arithmetic  415 us (31%)
  matrix products  331 us (24%)
  local copies, waits for them, and re-layouts  102 us (8%)
  between operations  15 us (1%)
    psum x1, waiting for transfers between devices, from_root(): return lax.psum(kept, axis)  211 us
    all_gather x1, waiting for transfers between devices, local(): pieces = lax.all_gather(corner, ('row', 'col'), axis=0, tiled=True)  209 us
    another operation x48, other arithmetic, block_cholesky(): diag_factor = jnp.linalg.cholesky(column[:BLK])  200 us
    another operation x32, other arithmetic, block_cholesky(): jax.scipy.linalg.solve_triangular(diag_factor, identity, lower=True)  178 us
    dot_general x15, matrix products, block_solve(): jnp.dot(result[:, :start], factor[start:start + BLK, :start].T, precision...  132 us
    dot_general x15, matrix products, block_cholesky(): jnp.dot(factor[start:, :start], factor[start:start + BLK, :start].T, prec...  77.6 us
    all_to_all x1, waiting for transfers between devices, local(): lax.all_to_all(outgoing, 'row', split_axis=1, concat_axis=1, tiled=True)  58.4 us
    dot_general x16, matrix products, block_solve(): jnp.dot(target, inverses[step].T, precision=lax.Precision.HIGHEST, prefer...  43.4 us
  transfers between devices with their start and end apart: 4, of which 3 were waited for; matrix products, arithmetic and copies ran while one was open for 40% of the time, Pallas kernels for 0%

commit v1 on v0

--- a/solution.py
+++ b/solution.py
@@ -117,7 +117,8 @@
         .reshape(front_rows, PW)
     )
     corner = assembled[: panel_rslots * BLK, : panel_cslots * BLK]
-    pieces = lax.all_gather(corner, ("row", "col"), axis=0, tiled=True)
+    outgoing_2 = jnp.stack([corner] * lax.axis_size(("row", "col")))
+    pieces = jnp.concatenate(lax.all_to_all(outgoing_2, ("row", "col"), 0, 0), axis=0)
     leading = (
         pieces.reshape(rows_n, cols_n, panel_rslots, BLK, panel_cslots, BLK)
         .transpose(2, 0, 3, 4, 1, 5)

time: 1360 us -> 1370 us (level)
  matrix products: 331 us -> 298 us
  waiting for transfers between devices: 479 us -> 511 us
    all_to_all x0 -> x1, waiting for transfers between devices: none -> 231 us  [local(): lax.all_to_all(outgoing_2, ('row', 'col'), 0, 0)]
    all_gather x1 -> x0, waiting for transfers between devices: 209 us -> none  [local(): pieces = lax.all_gather(corner, ('row', 'col'), axis=0, tiled=True)]
    dot_general x16, matrix products: 43.4 us -> 22.1 us  [block_solve(): jnp.dot(target, inverses[step].T, precision=lax.Precision.HIGHEST, prefer...]
    reshape x1 -> x0, local copies, waits for them, and re-layouts: 17.8 us -> none  [local(): pieces.reshape(rows_n, cols_n, panel_rslots, BLK, panel_cslots, BLK)]
    transpose x0 -> x1, local copies, waits for them, and re-layouts: none -> 17.7 us  [local(): leading = pieces.reshape(rows_n, cols_n, panel_rslots, BLK, panel_cslots,...]
  transfers between devices with their start and end apart: 4 -> 4, of which waited for: 3 -> 3; matrix products, arithmetic and copies ran while one was open for 40% -> 41% of each run, Pallas kernels for 0% -> 0%
where the time goes in v1:
time: 1370 us; the launch traced here: 1360 us
  waiting for transfers between devices  511 us (37%)
  other arithmetic  415 us (30%)
  matrix products  298 us (22%)
  local copies, waits for them, and re-layouts  107 us (8%)
  starting transfers between devices  16.3 us (1%)
  between operations  15.6 us (1%)
    all_to_all x1, waiting for transfers between devices, local(): lax.all_to_all(outgoing_2, ('row', 'col'), 0, 0)  231 us
    psum x1, waiting for transfers between devices, from_root(): return lax.psum(kept, axis)  221 us
    another operation x48, other arithmetic, block_cholesky(): diag_factor = jnp.linalg.cholesky(column[:BLK])  200 us
    another operation x32, other arithmetic, block_cholesky(): jax.scipy.linalg.solve_triangular(diag_factor, identity, lower=True)  178 us
    dot_general x15, matrix products, block_solve(): jnp.dot(result[:, :start], factor[start:start + BLK, :start].T, precision...  122 us
    dot_general x15, matrix products, block_cholesky(): jnp.dot(factor[start:, :start], factor[start:start + BLK, :start].T, prec...  77.6 us
    all_to_all x1, waiting for transfers between devices, local(): lax.all_to_all(outgoing, 'row', split_axis=1, concat_axis=1, tiled=True)  58.5 us
    dot_general x1, matrix products, local(): jnp.dot(factor_rows, column_rows.T, precision=lax.Precision.HIGHEST, pref...  31.4 us
  transfers between devices with their start and end apart: 4, of which 3 were waited for; matrix products, arithmetic and copies ran while one was open for 41% of the time, Pallas kernels for 0%

profile of v1, /device:TPU:1, one launch (start us, length us, event | category | flops | bytes accessed | tf_op | source)
XLA Modules:
  0.0 1363.2 jit_solution(4588088179376667469)
XLA Ops:
  18.3 58.5 %all-to-all-done = f32[2,8,128,512]{3,2,0,1:T(8,128)} async-done(((f32[2,8,128,512]{3,2,0,1:T(8,128)}), f32[2,8,128,512]{3,2,0,1:T(8,128)}, u32[]{:S(2)}, u32[]{:S(2)}) %all-to-all-start) | async-done | bytes 4194336 | tf_op jit(solution)/shard_map/all_to_all | solution.py:83
  108.7 10.3 all-to-all-start.1
  125.5 230.8 %all-to-all-done.1 = f32[128,256,128]{2,1,0:T(8,128)} async-done(((f32[128,256,128]{2,1,0:T(8,128)}), f32[128,256,128]{2,1,0:T(8,128)}, u32[]{:S(2)}, u32[]{:S(2)}) %all-to-all-start.1) | async-done | bytes 16777248 | tf_op jit(solution)/shard_map/all_to_all | solution.py:121
  356.3 17.7 %copy.160 = f32[2,8,128,1,16,128]{2,1,0,5,4,3:T(8,128)} copy(f32[2,8,128,1,16,128]{5,2,0,4,1,3:T(8,128)} %bitcast.18) | data formatting | bytes 33554432 | tf_op jit(solution)/shard_map/transpose | solution.py:124
  374.0 18.4 %reshape.1454 = f32[2048,2048]{0,1:T(8,128)} reshape(f32[2,8,128,1,16,128]{2,1,0,5,4,3:T(8,128)} %copy.160) | data formatting | bytes 33554432 | tf_op jit(solution)/shard_map/reshape | solution.py:125
  394.3 11.7 cholesky.254
  407.4 9.8 custom-call.20
  431.7 11.9 cholesky.265
  445.6 9.8 custom-call.21
  462.2 11.7 cholesky.276
  476.0 10.0 custom-call.22
  493.7 11.7 cholesky.287
  507.4 9.8 custom-call.23
  525.9 11.7 cholesky.298
  539.7 9.8 custom-call.24
  558.1 11.7 cholesky.309
  571.8 9.8 custom-call.25
  590.9 11.7 cholesky.320
  604.6 9.8 custom-call.26
  623.4 12.1 cholesky.331
  637.6 9.8 custom-call.27
  656.6 11.9 cholesky.342
  670.4 9.8 custom-call.28
  688.7 11.9 cholesky.353
  702.7 9.8 custom-call.29
  720.9 11.7 cholesky.364
  734.7 10.2 custom-call.30
  752.6 11.7 cholesky.375
  766.3 9.8 custom-call.31
  783.5 11.7 cholesky.386
  797.2 9.8 custom-call.32
  813.1 11.9 cholesky.397
  827.1 9.8 custom-call.33
  842.1 11.7 cholesky.408
  855.8 10.2 custom-call.34
  870.0 11.7 cholesky.419
  883.8 9.8 custom-call.35
  952.7 8.9 fusion.119
  963.0 9.8 fusion.96
  974.1 11.1 fusion.122
  986.6 11.5 fusion.72
  999.4 12.6 fusion.75
  1013.4 13.4 fusion.125
  1028.2 14.3 %fusion.78 = f32[1024,128]{1,0:T(8,128)S(1)} fusion(f32[1024,2048]{0,1:T(8,128)S(1)} %fusion.99, f32[2048,2048]{1,0:T(8,128)} %get-tuple-element.575, f32[1280,2048]{1,0:T(8,128)S(1)} %copy-done.4), kind=kOutput, calls=%fused_computation.84 | convolution fusion | flops 3020029952 | bytes 9895936 | tf_op jit(solution)/shard_map/dot_general | solution.py:53
  1052.9 13.3 reshape.1458
  1066.1 21.0 %fusion.10 = f32[5,128,2048]{1,0,2:T(8,128)} fusion(pred[]{:T(512)S(6)} %eq.132, f32[5,2,128,2048]{2,1,0,3:T(2,128)} %reshape.1458, s32[]{:T(128)S(6)} %select_n.110), kind=kLoop, calls=%fused_computation.14 | loop fusion | flops 1310720 | bytes 10485765 | tf_op jit(solution)/shard_map/jit(_where)/select_n | solution.py:11
  1103.1 221.5 %all-reduce.4.cloned.1.call-done = f32[640,2048]{0,1:T(8,128)} async-done(((f32[640,2048]{0,1:T(8,128)}), f32[640,2048]{0,1:T(8,128)}) %all-reduce.4.cloned.1.call-update) | async-done | bytes 5242896 | tf_op jit(solution)/shard_map/psum | solution.py:12
  1324.6 31.4 %fusion.33 = f32[1280,640]{1,0:T(8,128)} fusion(f32[1280,640]{1,0:T(8,128)} %copy-done.5, f32[640,2048]{0,1:T(8,128)} %all-reduce.4.cloned.1.call-done, pred[640]{0:T(1024)(128)(4,1)S(1)} %fusion.278, pred[1280]{0:T(1024)(128)(4,1)S(1)} %fusion.274, f32[1024,2048]{0,1:T(8,128)} %copy-done, f32[256,2048]{0,1:T(8,128)S(1)} %copy-done.3), kind=kOutput, calls=%fused_computation.39 | convolution fusion | flops 20137738240 | bytes 22284160 | tf_op jit(solution)/shard_map/dot_general | solution.py:139
  (227 shorter events, 296.9 us)
Async XLA Ops:
  7.2 10.8 copy-start.7
  11.9 64.8 %all-to-all-start = ((f32[2,8,128,512]{3,2,0,1:T(8,128)}), f32[2,8,128,512]{3,2,0,1:T(8,128)}, u32[]{:S(2)}, u32[]{:S(2)}) async-start(f32[2,8,128,512]{3,2,0,1:T(8,128)} %copy.155), calls=%async_computation | async-start | bytes 8388608 | tf_op jit(solution)/shard_map/all_to_all | solution.py:83
  89.3 9.7 copy-start.6
  100.9 23.7 %copy-start.5 = (f32[1280,640]{1,0:T(8,128)}, f32[1280,640]{1,0:T(8,128)S(1)}, u32[]{:S(2)}) copy-start(f32[1280,640]{1,0:T(8,128)S(1)} %bitcast_add_fusion) | copy-start | bytes 9830404
  108.7 247.6 %all-to-all-start.1 = ((f32[128,256,128]{2,1,0:T(8,128)}), f32[128,256,128]{2,1,0:T(8,128)}, u32[]{:S(2)}, u32[]{:S(2)}) async-start(f32[128,256,128]{2,1,0:T(8,128)} %stack.2), calls=%async_computation.1 | async-start | bytes 33554432 | tf_op jit(solution)/shard_map/all_to_all | solution.py:121
  119.0 778.8 %all-gather.2.cloned.1.call-start = ((), (), s32[]{:S(2)}) async-start(), calls=%async_computation.2 | async-start | bytes 11141120 | tf_op jit(solution)/shard_map/all_gather | solution.py:113
  125.5 1199.1 %all-reduce.4.cloned.1.call-start = ((), (), s32[]{:S(2)}) async-start(), calls=%async_computation.3 | async-start | bytes 10485760 | tf_op jit(solution)/shard_map/psum | solution.py:12
  895.3 2.5 copy-start.1
  897.8 6.8 copy-start.4
  1043.1 3.3 copy-start
  1087.1 7.2 copy-start.2
  1097.8 226.8 %copy-start.3 = (f32[256,2048]{0,1:T(8,128)S(1)}, f32[256,2048]{0,1:T(8,128)}, u32[]{:S(2)}) copy-start(f32[256,2048]{0,1:T(8,128)} %copy.215) | copy-start | bytes 6291460
Sparse Core Ops, SparseCore 0:
  125.6 269.2 all-gather.1
  1094.4 230.1 all-reduce.3
